TPU v7x, 32 devices: a whole 2x2x4 slice. The times are simulated.
32 devices in a mesh: group: 4 (over y, core), seq: 4 (over z), mp: 2 (over x).
Axes of the slice: x: 2, y: 2, z: 4, core: 2. Of those that a mesh axis runs over, the one named last changes fastest.
Arguments:
- gen_hidden: bfloat16 [4, 64, 2048], P('seq', ('group', 'mp')), may hold values from -6 to 6
- gen_gain: float32 [2048], replicated, may hold values from 0.5 to 1.5
- head_weight: bfloat16 [2048, 64], replicated, may hold values from -0.125 to 0.125
- noise: float32 [4, 64, 64], P('seq', ('group', 'mp')), may hold values from -6 to 6
- timestep: int32 [1], replicated, may hold values from 20 to 980
- stream: bfloat16 [4, 64, 5120], P('seq', None, 'mp'), may hold values from -60 to 60
- patch_weight: bfloat16 [64, 5120], P(None, 'mp'), may hold values from -0.75 to 0.75
- conditions: float32 [4, 5120], P('group', 'mp'), may hold values from -6 to 6
- teacher_qkv: bfloat16 [5120, 3, 4, 128], P('mp', None, 'seq'), may hold values from -0.078125 to 0.078125
- teacher_out: bfloat16 [4, 128, 64], P('seq'), may hold values from -0.25 to 0.25
- fake_qkv: bfloat16 [5120, 3, 4, 128], P('mp', None, 'seq'), may hold values from -0.078125 to 0.078125
- fake_out: bfloat16 [4, 128, 64], P('seq'), may hold values from -0.25 to 0.25
Outputs:
- score_gap: float32 [4, 64, 64], P('seq', ('group', 'mp'))
- grad_hidden: bfloat16 [4, 64, 2048], P('seq', ('group', 'mp'))
All inputs are finite; a program needn't handle non-finite values.
Results may differ from a plain program's by a relative error of at most 0.02.
The roundings to bfloat16 on the way count: a program that leaves them out, or rounds other values in their place, can miss the bound.
Values may be sent and summed in bfloat16 or wider, within the bound.
A program may use at most 64 MiB of HBM per device.

v0:
```python
import jax
import jax.numpy as jnp
from jax import lax
from jax.sharding import PartitionSpec as P

guidance = 3.0
eps = 1e-06


def local(
    gen_hidden,
    gen_gain,
    head_weight,
    noise,
    timestep,
    stream,
    patch_weight,
    conditions,
    teacher_qkv,
    teacher_out,
    fake_qkv,
    fake_out,
):
    n_group = lax.axis_size("group")
    n_seq = lax.axis_size("seq")
    n_mp = lax.axis_size("mp")
    group_id = lax.axis_index("group")
    tok_dev = stream.shape[1]
    ds_loc = stream.shape[2]
    head_dim = teacher_qkv.shape[3]
    per_dev = gen_hidden.shape[1]
    width = 3 * head_dim
    hidden = gen_hidden[0].astype(jnp.float32)
    rms = 1.0 / jnp.sqrt(jnp.mean(hidden * hidden, axis=-1, keepdims=True) + eps)
    normed = (hidden * rms * gen_gain[None, :]).astype(jnp.bfloat16)
    clean = jnp.dot(normed, head_weight, preferred_element_type=jnp.float32)
    sigma = timestep[0].astype(jnp.float32) / 1000.0
    noised = ((1.0 - sigma) * clean + sigma * noise[0]).astype(jnp.bfloat16)
    is_fake = group_id == 0
    qkv_weight = jnp.where(is_fake, fake_qkv, teacher_qkv).reshape(ds_loc, width)
    out_weight = jnp.where(is_fake, fake_out, teacher_out)[0]
    coeff = jnp.where(
        group_id == 0,
        1.0,
        jnp.where(group_id == 1, -guidance, jnp.where(group_id == 2, guidance - 1.0, 0.0)),
    )
    cond_row = conditions[0][None, None, :]
    block_lat = lax.all_gather(noised, ("group", "mp"), axis=0, tiled=True)
    embedded = jnp.dot(block_lat, patch_weight, preferred_element_type=jnp.float32)
    rows = (stream[0].astype(jnp.float32) + embedded + cond_row[0]).astype(jnp.bfloat16)[None]
    queries_count = n_group * n_seq * per_dev
    piece = lax.all_gather(rows, "seq", axis=0, tiled=True)
    product = jnp.dot(piece.reshape(-1, ds_loc), qkv_weight, preferred_element_type=jnp.float32)
    partial_value = product.reshape(piece.shape[0], tok_dev, width)
    kv_part = partial_value[:, :, head_dim:].reshape(n_seq * tok_dev, 2 * head_dim)
    keys_vals = lax.psum(kv_part.astype(jnp.bfloat16), "mp")
    query_part = partial_value[:, :, :head_dim].reshape(n_seq, n_group, n_mp, per_dev, head_dim)
    query_part = query_part.transpose(2, 1, 0, 3, 4).reshape(n_mp * queries_count, head_dim)
    queries = lax.psum_scatter(
        query_part.astype(jnp.bfloat16), "mp", scatter_dimension=0, tiled=True
    )
    keys = keys_vals[:, :head_dim]
    values = keys_vals[:, head_dim:]
    scores = jnp.dot(queries, keys.T, preferred_element_type=jnp.float32) / jnp.sqrt(
        jnp.float32(head_dim)
    )
    top = jnp.max(scores, axis=-1, keepdims=True)
    expo = jnp.exp(scores - top)
    probs = (expo / jnp.sum(expo, axis=-1, keepdims=True)).astype(jnp.bfloat16)
    heads = jnp.dot(probs, values, preferred_element_type=jnp.float32).astype(jnp.bfloat16)
    weighted = coeff * jnp.dot(heads, out_weight, preferred_element_type=jnp.float32)
    score_gap = lax.psum_scatter(weighted, ("group", "seq"), scatter_dimension=0, tiled=True)
    gap_in = score_gap.astype(jnp.bfloat16)
    grad_normed = jnp.dot(gap_in, head_weight.T, preferred_element_type=jnp.float32)
    scaled = hidden * rms
    grad_gain = grad_normed * gen_gain[None, :]
    grad_hidden = rms * (grad_gain - scaled * jnp.mean(scaled * grad_gain, axis=-1, keepdims=True))
    return (score_gap[None], grad_hidden.astype(jnp.bfloat16)[None])


def solution(mesh):
    placed = (
        P("seq", ("group", "mp"), None),
        P(),
        P(),
        P("seq", ("group", "mp"), None),
        P(),
        P("seq", None, "mp"),
        P(None, "mp"),
        P("group", "mp"),
        P("mp", None, "seq", None),
        P("seq", None, None),
        P("mp", None, "seq", None),
        P("seq", None, None),
    )
    return jax.shard_map(
        local,
        mesh=mesh,
        in_specs=placed,
        out_specs=(P("seq", ("group", "mp"), None), P("seq", ("group", "mp"), None)),
        check_vma=False,
    )
```

profile of v0, /device:TPU:0, one launch (start us, length us, event | category | flops | bytes accessed | tf_op | source)
XLA Modules:
  0.0 171.2 jit_solution(14491425108216744386)
XLA Ops:
  7.2 0.0 copy-start
  7.2 0.0 all-gather.3.cloned.1.call-start
  7.2 0.9 fusion.13
  8.8 1.2 fusion.3
  10.0 16.9 %all_gather.6 = bf16[64,64]{1,0:T(8,128)(2,1)S(1)} all-gather(bf16[8,64]{1,0:T(8,128)(2,1)S(1)} %fusion.3), channel_id=1, replica_groups=mesh['group'=4,'seq'=4,'mp'=2] {'group','mp'}, dimensions={0}, use_global_device_ids=true | all-gather | bytes 9216 | tf_op jit(solution)/shard_map/all_gather | solution.py:48
  27.0 0.7 reduce
  27.7 0.0 copy-done
  27.7 1.9 %fusion.1 = bf16[64,2560]{1,0:T(8,128)(2,1)} fusion(bf16[64,64]{1,0:T(8,128)(2,1)S(1)} %all_gather.6, bf16[64,2560]{1,0:T(8,128)(2,1)S(1)} %copy-done, bf16[1,64,2560]{2,1,0:T(8,128)(2,1)} %param.17, f32[2560]{0:T(1024)S(1)} %reduce), kind=kOutput, calls=%fused_computation.2 | convolution fusion | flops 21626880 | bytes 1001472 | tf_op jit(solution)/shard_map/dot_general | solution.py:49
  29.6 0.0 all-gather.3.cloned.1.call-update
  29.7 0.0 all-reduce.3.cloned.1.call-start
  29.7 2.7 %copy.18 = bf16[2560,3,1,128]{0,3,1,2:T(8,128)(2,1)S(1)} copy(bf16[2560,3,1,128]{3,0,2,1:T(8,128)(2,1)} %param.22) | data formatting | bytes 3932160 | tf_op args[10]
  32.4 4.0 %copy.19 = bf16[2560,3,1,128]{0,3,1,2:T(8,128)(2,1)} copy(bf16[2560,3,1,128]{3,0,2,1:T(8,128)(2,1)} %param.20) | data formatting | bytes 3932160 | tf_op args[8]
  36.4 1.5 broadcast_select_fusion
  37.9 25.4 %all-gather.3.cloned.1.call-done = bf16[256,2560]{1,0:T(8,128)(2,1)} async-done(((bf16[64,2560]{1,0:T(8,128)(2,1)}), bf16[256,2560]{1,0:T(8,128)(2,1)}) %all-gather.3.cloned.1.call-update) | async-done | bytes 1310736 | tf_op jit(solution)/shard_map/all_gather | solution.py:52
  63.3 0.0 copy-start.3
  63.3 2.9 %convolution_convert_fusion = bf16[4,64,384]{2,1,0:T(8,128)(2,1)S(1)} fusion(bf16[4,64,2560]{2,1,0:T(8,128)(2,1)} %bitcast.43, bf16[2560,384,1]{0,1,2:T(8,128)(2,1)} %bitcast.39), kind=kOutput, calls=%fused_computation.5 | convolution fusion | flops 503414784 | bytes 3473408 | tf_op jit(solution)/shard_map/dot_general | solution.py:53
  66.1 0.7 slice.19
  66.8 0.0 all-reduce.3.cloned.1.call-update
  66.8 0.0 reduce-scatter.2.cloned.1.call-start
  66.9 0.6 copy.21
  67.5 0.0 reduce-scatter.2.cloned.1.call-update
  67.6 0.6 dynamic-slice
  68.8 18.6 %all-reduce.3.cloned.1.call-done = bf16[256,256]{1,0:T(8,128)(2,1)} async-done(((bf16[256,256]{1,0:T(8,128)(2,1)}), bf16[256,256]{1,0:T(8,128)(2,1)}) %all-reduce.3.cloned.1.call-update) | async-done | bytes 131088 | tf_op jit(solution)/shard_map/psum | solution.py:56
  87.4 12.1 %reduce-scatter.2.cloned.1.call-done = bf16[128,128]{1,0:T(8,128)(2,1)} async-done(((bf16[256,128]{1,0:T(8,128)(2,1)}), bf16[128,128]{1,0:T(8,128)(2,1)}) %reduce-scatter.2.cloned.1.call-update) | async-done | bytes 32784 | tf_op jit(solution)/shard_map/reduce_scatter | solution.py:59
  99.5 1.1 fusion.30
  100.6 0.2 fusion.4
  100.9 1.2 convolution_multiply_fusion.2
  102.0 61.1 %all-reduce = f32[128,64]{1,0:T(8,128)S(1)} all-reduce(f32[128,64]{1,0:T(8,128)S(1)} %convolution_multiply_fusion.2), channel_id=4, replica_groups=mesh['group'=4,'seq'=4,'mp'=2] {'group','seq'}, use_global_device_ids=true, to_apply=%region_5.6.clone | all-reduce | flops 8192 | bytes 65536
  163.1 0.0 copy-done.3
  163.1 0.3 fusion.9
  163.4 0.6 dynamic-slice_bitcast_fusion
  164.0 0.7 fusion.21
  (13 shorter events, 0.0 us)
Async XLA Ops:
  7.2 20.5 %copy-start = (bf16[64,2560]{1,0:T(8,128)(2,1)S(1)}, bf16[64,2560]{1,0:T(8,128)(2,1)}, u32[]{:S(2)}) copy-start(bf16[64,2560]{1,0:T(8,128)(2,1)} %param.18) | copy-start | bytes 983044
  7.2 56.1 %all-gather.3.cloned.1.call-start = ((), (), s32[]{:S(2)}) async-start(), calls=%async_computation.3 | async-start | bytes 1638400 | tf_op jit(solution)/shard_map/all_gather | solution.py:52
  29.7 57.8 %all-reduce.3.cloned.1.call-start = ((), (), s32[]{:S(2)}) async-start(), calls=%async_computation.2 | async-start | bytes 262144 | tf_op jit(solution)/shard_map/psum | solution.py:56
  63.3 4.3 %copy-start.6 = (u32[32]{0:T(128)S(1)}, u32[32]{0:T(128)}, u32[]{:S(2)}) copy-start(u32[32]{0:T(128)} %constant.45) | copy-start | bytes 388
  63.3 37.6 %copy-start.4 = (bf16[1,128,64]{1,2,0:T(8,128)(2,1)S(1)}, bf16[1,128,64]{1,2,0:T(8,128)(2,1)}, u32[]{:S(2)}) copy-start(bf16[1,128,64]{1,2,0:T(8,128)(2,1)} %param.23) | copy-start | bytes 49156
  63.3 37.6 %copy-start.5 = (bf16[1,128,64]{1,2,0:T(8,128)(2,1)S(1)}, bf16[1,128,64]{1,2,0:T(8,128)(2,1)}, u32[]{:S(2)}) copy-start(bf16[1,128,64]{1,2,0:T(8,128)(2,1)} %param.21) | copy-start | bytes 49156
  63.3 99.9 %copy-start.1 = (bf16[1,8,2048]{2,1,0:T(8,128)(2,1)S(1)}, bf16[1,8,2048]{2,1,0:T(8,128)(2,1)}, u32[]{:S(2)}) copy-start(bf16[1,8,2048]{2,1,0:T(8,128)(2,1)} %param.12) | copy-start | bytes 98308
  63.3 99.9 %copy-start.2 = (bf16[2048,64]{0,1:T(8,128)(2,1)S(1)}, bf16[2048,64]{0,1:T(8,128)(2,1)}, u32[]{:S(2)}) copy-start(bf16[2048,64]{0,1:T(8,128)(2,1)} %param.14) | copy-start | bytes 786436
  63.3 99.9 %copy-start.3 = (f32[2048]{0:T(1024)S(1)}, f32[2048]{0:T(1024)}, u32[]{:S(2)}) copy-start(f32[2048]{0:T(1024)} %param.13) | copy-start | bytes 24580
  66.8 32.7 %reduce-scatter.2.cloned.1.call-start = ((), (), s32[]{:S(2)}) async-start(), calls=%async_computation.1 | async-start | bytes 98304 | tf_op jit(solution)/shard_map/reduce_scatter | solution.py:59
Sparse Core Ops, SparseCore 0:
  29.8 33.4 all-gather.2
  66.9 20.4 all-reduce.2
  89.6 9.8 reduce-scatter.1
where the time goes:
time: 172 us; the launch traced here: 171 us
  blocking collectives  78 us (45%)
  waiting for transfers between devices  56.1 us (33%)
  between operations  15.2 us (9%)
  local copies, waits for them, and re-layouts  9.21 us (5%)
  matrix products  8.57 us (5%)
  other arithmetic  4.04 us (2%)
    unnamed x1, blocking collectives  61.1 us
    all_gather x1, waiting for transfers between devices, local(): piece = lax.all_gather(rows, 'seq', axis=0, tiled=True)  25.4 us
    psum x1, waiting for transfers between devices, local(): keys_vals = lax.psum(kv_part.astype(jnp.bfloat16), 'mp')  18.6 us
    all_gather x1, blocking collectives, local(): block_lat = lax.all_gather(noised, ('group', 'mp'), axis=0, tiled=True)  16.9 us
    reduce_scatter x1, waiting for transfers between devices, local(): lax.psum_scatter(query_part.astype(jnp.bfloat16), 'mp', scatter_dimension...  12.1 us
    unnamed x17, local copies, waits for them, and re-layouts  7.3 us
  transfers between devices with their start and end apart: 3, of which 3 were waited for; matrix products, arithmetic and copies ran while one was open for 5% of the time, Pallas kernels for 0%

commit v1 on v0

--- a/solution.py
+++ b/solution.py
@@ -1,10 +1,340 @@
+import functools
+
 import jax
 import jax.numpy as jnp
 from jax import lax
+from jax.experimental import pallas as pl
+from jax.experimental.pallas import tpu as pltpu
 from jax.sharding import PartitionSpec as P
 
 guidance = 3.0
 eps = 1e-06
+MESH = pl.DeviceIdType.MESH
+F32 = jnp.float32
+BF16 = jnp.bfloat16
+EVALS = 3
+
+
+def kernel(
+    sizes,
+    hid_ref,
+    gain_ref,
+    head_t_ref,
+    noise_ref,
+    time_ref,
+    stream_ref,
+    patch_ref,
+    cond_ref,
+    teacher_ref,
+    teacher_out_ref,
+    fake_ref,
+    fake_out_ref,
+    gap_ref,
+    grad_ref,
+    latents,
+    rows,
+    conds,
+    w_fake,
+    w_teach,
+    part_out,
+    part_in,
+    keys_vals,
+    vel_out,
+    vel_in,
+    local_sem,
+    lat_send,
+    lat_recv,
+    cond_send,
+    cond_recv,
+    row_send,
+    row_recv,
+    part_send,
+    part_recv,
+    kv_send,
+    kv_recv,
+    vel_send,
+    vel_recv,
+):
+    n_group, n_seq, n_mp, n_chunk = sizes
+    g = lax.axis_index("group")
+    s = lax.axis_index("seq")
+    m = lax.axis_index("mp")
+    per_dev = hid_ref.shape[1]
+    ds_loc = stream_ref.shape[2]
+    share = n_mp * per_dev
+    tokens = n_seq * share
+    queries = n_seq * per_dev
+    head_dim = teacher_ref.shape[2]
+    chunk = ds_loc // n_chunk
+
+    def at_seq(d):
+        return lax.rem(s + d, n_seq)
+
+    def at_mp(d):
+        return lax.rem(m + d, n_mp)
+
+    def at_group(d):
+        return lax.rem(g + d, n_group)
+
+    plane = [(ds, dm) for ds in range(n_seq) for dm in range(n_mp) if ds or dm]
+
+    def push(src, dst, send, recv, device):
+        copy = pltpu.make_async_remote_copy(
+            src_ref=src, dst_ref=dst, send_sem=send, recv_sem=recv, device_id=device, device_id_type=MESH
+        )
+        copy.start()
+        return copy
+
+    barrier = pltpu.get_barrier_semaphore()
+    for ds, dm in plane:
+        pl.semaphore_signal(barrier, inc=1, device_id=(g, at_seq(ds), at_mp(dm)), device_id_type=MESH)
+    for d in range(1, n_group):
+        pl.semaphore_signal(barrier, inc=1, device_id=(at_group(d), s, m), device_id_type=MESH)
+
+    my_rows = pl.ds(pl.multiple_of(g * share, share), share)
+    own = [
+        pltpu.make_async_copy(stream_ref.at[0, my_rows, :], rows.at[s], local_sem.at[0]),
+        pltpu.make_async_copy(cond_ref, conds.at[g], local_sem.at[1]),
+    ]
+    for j in range(3):
+        cols = pl.ds(j * head_dim, head_dim)
+        own.append(pltpu.make_async_copy(fake_ref.at[j], w_fake.at[:, cols], local_sem.at[2 + j]))
+        own.append(pltpu.make_async_copy(teacher_ref.at[j], w_teach.at[:, cols], local_sem.at[5 + j]))
+    for copy in own:
+        copy.start()
+
+    hidden = hid_ref[0].astype(F32)
+    gain = gain_ref[...]
+    rms = 1.0 / jnp.sqrt(jnp.mean(hidden * hidden, axis=-1, keepdims=True) + eps)
+    normed = (hidden * rms * gain).astype(BF16)
+    clean = lax.dot_general(normed, head_t_ref[...], (((1,), (1,)), ((), ())), preferred_element_type=F32)
+    sigma = jnp.full(clean.shape, time_ref[0], jnp.int32).astype(F32) / 1000.0
+    noised = ((1.0 - sigma) * clean + sigma * noise_ref[0]).astype(BF16)
+    latents[s, m] = noised.astype(F32)
+
+    pl.semaphore_wait(barrier, len(plane) + n_group - 1)
+
+    lat_copies = []
+    for i, (ds, dm) in enumerate(plane):
+        lat_copies.append(
+            push(latents.at[s, m], latents.at[s, m], lat_send.at[i], lat_recv.at[i], (g, at_seq(ds), at_mp(dm)))
+        )
+    cond_copies = []
+    row_copies = []
+    for c in range(n_chunk):
+        cols = pl.ds(c * chunk, chunk)
+        group_of = []
+        for d in range(1, n_seq):
+            group_of.append(
+                push(
+                    stream_ref.at[0, my_rows, cols],
+                    rows.at[s, :, cols],
+                    row_send.at[c, d - 1],
+                    row_recv.at[c, d - 1],
+                    (g, at_seq(d), m),
+                )
+            )
+        row_copies.append(group_of)
+        if c == 0:
+            for d in range(1, n_group):
+                cond_copies.append(
+                    push(cond_ref, conds.at[g], cond_send.at[d - 1], cond_recv.at[d - 1], (at_group(d), s, m))
+                )
+
+    for copy in lat_copies:
+        copy.wait_recv()
+    lat_all = latents[...].reshape(tokens, -1).astype(BF16)
+    for copy in own:
+        copy.wait()
+    for copy in cond_copies:
+        copy.wait_recv()
+
+    acc_fake = None
+    acc_teach = None
+    for c in range(n_chunk):
+        cols = pl.ds(c * chunk, chunk)
+        for copy in row_copies[c]:
+            copy.wait_recv()
+        base = rows[:, :, cols].reshape(tokens, chunk).astype(F32) + jnp.dot(
+            lat_all, patch_ref[:, cols], preferred_element_type=F32
+        )
+        layer = [(base + conds[e, :, cols]).astype(BF16) for e in range(EVALS)]
+        fake = jnp.dot(layer[0], w_fake[cols, :], preferred_element_type=F32)
+        teach = jnp.dot(jnp.concatenate(layer[1:], axis=0), w_teach[cols, :], preferred_element_type=F32)
+        acc_fake = fake if c == 0 else acc_fake + fake
+        acc_teach = teach if c == 0 else acc_teach + teach
+
+    partial = [acc_fake, acc_teach[:tokens], acc_teach[tokens:]]
+    part_copies = []
+    for e in range(EVALS):
+        q_part = partial[e][:, :head_dim].reshape(n_seq, n_mp, per_dev, head_dim)
+        k_part = partial[e][:, head_dim : 2 * head_dim].astype(BF16)
+        v_part = partial[e][:, 2 * head_dim :].astype(BF16)
+        for k in range(n_mp):
+            part_out[e, k, :tokens] = k_part
+            part_out[e, k, tokens : 2 * tokens] = v_part
+            part_out[e, k, 2 * tokens :] = q_part[:, k].reshape(queries, head_dim).astype(BF16)
+        part_copies.append(
+            [
+                push(
+                    part_out.at[e, at_mp(d)],
+                    part_in.at[e, d - 1],
+                    part_send.at[e, d - 1],
+                    part_recv.at[e, d - 1],
+                    (g, s, at_mp(d)),
+                )
+                for d in range(1, n_mp)
+            ]
+        )
+
+    kv_copies = []
+    queries_of = []
+    for e in range(EVALS):
+        total = part_out[e, m].astype(F32)
+        for d in range(1, n_mp):
+            part_copies[e][d - 1].wait_recv()
+            total = total + part_in[e, d - 1].astype(F32)
+        total = total.astype(BF16)
+        keys_vals[e, g] = total[: 2 * tokens]
+        queries_of.append(total[2 * tokens :])
+        kv_copies.append(
+            [
+                push(
+                    keys_vals.at[e, g],
+                    keys_vals.at[e, g],
+                    kv_send.at[e, d - 1],
+                    kv_recv.at[e, d - 1],
+                    (at_group(d), s, m),
+                )
+                for d in range(1, n_group)
+            ]
+        )
+
+    coeff = (1.0, -guidance, guidance - 1.0)
+    velocity = None
+    for e in range(EVALS):
+        for copy in kv_copies[e]:
+            copy.wait_recv()
+        keys = keys_vals[e, :, :tokens].reshape(n_group * tokens, head_dim)
+        values = keys_vals[e, :, tokens:].reshape(n_group * tokens, head_dim)
+        scores = lax.dot_general(
+            queries_of[e], keys, (((1,), (1,)), ((), ())), preferred_element_type=F32
+        ) / jnp.sqrt(F32(head_dim))
+        top = jnp.max(scores, axis=-1, keepdims=True)
+        expo = jnp.exp(scores - top)
+        probs = (expo / jnp.sum(expo, axis=-1, keepdims=True)).astype(BF16)
+        heads = jnp.dot(probs, values, preferred_element_type=F32).astype(BF16)
+        out_t = fake_out_ref[0] if e == 0 else teacher_out_ref[0]
+        term = coeff[e] * lax.dot_general(heads, out_t, (((1,), (1,)), ((), ())), preferred_element_type=F32)
+        velocity = term if e == 0 else velocity + term
+
+    vel_out[...] = velocity.reshape(n_seq, per_dev, -1)
+    vel_copies = [
+        push(vel_out.at[at_seq(d)], vel_in.at[s], vel_send.at[d - 1], vel_recv.at[d - 1], (g, at_seq(d), m))
+        for d in range(1, n_seq)
+    ]
+    vel_in[s] = vel_out[s]
+    scaled = hidden * rms
+    for copy in vel_copies:
+        copy.wait_recv()
+    gap = vel_in[0]
+    for k in range(1, n_seq):
+        gap = gap + vel_in[k]
+    gap_ref[0] = gap
+    grad_normed = jnp.dot(gap.astype(BF16), head_t_ref[...], preferred_element_type=F32)
+    grad_gain = grad_normed * gain
+    grad = rms * (grad_gain - scaled * jnp.mean(scaled * grad_gain, axis=-1, keepdims=True))
+    grad_ref[0] = grad.astype(BF16)
+
+    for copy in lat_copies + cond_copies + vel_copies:
+        copy.wait_send()
+    for copies in row_copies + part_copies + kv_copies:
+        for copy in copies:
+            copy.wait_send()
+
+
+def fused(
+    gen_hidden,
+    gen_gain,
+    head_weight,
+    noise,
+    timestep,
+    stream,
+    patch_weight,
+    conditions,
+    teacher_qkv,
+    teacher_out,
+    fake_qkv,
+    fake_out,
+):
+    n_group = lax.axis_size("group")
+    n_seq = lax.axis_size("seq")
+    n_mp = lax.axis_size("mp")
+    per_dev = gen_hidden.shape[1]
+    lat = head_weight.shape[1]
+    ds_loc = stream.shape[2]
+    head_dim = teacher_qkv.shape[3]
+    share = n_mp * per_dev
+    tokens = n_seq * share
+    queries = n_seq * per_dev
+    width = 3 * head_dim
+    n_chunk = ds_loc // 512
+    packed = 2 * tokens + queries
+    n_plane = n_seq * n_mp - 1
+    vmem = pl.BlockSpec(memory_space=pltpu.VMEM)
+    hbm = pl.BlockSpec(memory_space=pl.ANY)
+    smem = pl.BlockSpec(memory_space=pltpu.SMEM)
+    dma = pltpu.SemaphoreType.DMA
+    return pl.pallas_call(
+        functools.partial(kernel, (n_group, n_seq, n_mp, n_chunk)),
+        out_shape=(
+            jax.ShapeDtypeStruct((1, per_dev, lat), F32),
+            jax.ShapeDtypeStruct(gen_hidden.shape, BF16),
+        ),
+        in_specs=[vmem, vmem, vmem, vmem, smem, hbm, vmem, vmem, hbm, vmem, hbm, vmem],
+        out_specs=(vmem, vmem),
+        scratch_shapes=[
+            pltpu.VMEM((n_seq, n_mp, per_dev, lat), F32),
+            pltpu.VMEM((n_seq, share, ds_loc), BF16),
+            pltpu.VMEM((n_group, 1, ds_loc), F32),
+            pltpu.VMEM((ds_loc, width), BF16),
+            pltpu.VMEM((ds_loc, width), BF16),
+            pltpu.VMEM((EVALS, n_mp, packed, head_dim), BF16),
+            pltpu.VMEM((EVALS, n_mp - 1, packed, head_dim), BF16),
+            pltpu.VMEM((EVALS, n_group, 2 * tokens, head_dim), BF16),
+            pltpu.VMEM((n_seq, per_dev, lat), F32),
+            pltpu.VMEM((n_seq, per_dev, lat), F32),
+            dma((8,)),
+            dma((n_plane,)),
+            dma((n_plane,)),
+            dma((n_group - 1,)),
+            dma((n_group - 1,)),
+            dma((n_chunk, n_seq - 1)),
+            dma((n_chunk, n_seq - 1)),
+            dma((EVALS, n_mp - 1)),
+            dma((EVALS, n_mp - 1)),
+            dma((EVALS, n_group - 1)),
+            dma((EVALS, n_group - 1)),
+            dma((n_seq - 1,)),
+            dma((n_seq - 1,)),
+        ],
+        compiler_params=pltpu.CompilerParams(
+            collective_id=0, has_side_effects=True, vmem_limit_bytes=40 * 1024 * 1024
+        ),
+    )(
+        gen_hidden,
+        gen_gain.reshape(1, -1),
+        head_weight.T,
+        noise,
+        timestep,
+        stream,
+        patch_weight,
+        conditions,
+        teacher_qkv[:, :, 0, :].transpose(1, 0, 2),
+        teacher_out.transpose(0, 2, 1),
+        fake_qkv[:, :, 0, :].transpose(1, 0, 2),
+        fake_out.transpose(0, 2, 1),
+    )
 
 
 def local(
@@ -93,8 +423,18 @@
         P("mp", None, "seq", None),
         P("seq", None, None),
     )
+    n_group, n_seq, n_mp = mesh.shape["group"], mesh.shape["seq"], mesh.shape["mp"]
+
+    def part(*arrays):
+        per_dev, ds_loc = arrays[0].shape[1], arrays[5].shape[2]
+        tiled = per_dev % 8 == 0 and n_mp * per_dev % 16 == 0 and n_seq * per_dev % 16 == 0
+        small = n_group > 1 and n_seq > 1 and n_mp > 1 and n_group >= EVALS
+        if tiled and small and ds_loc % 512 == 0:
+            return fused(*arrays)
+        return local(*arrays)
+
     return jax.shard_map(
-        local,
+        part,
         mesh=mesh,
         in_specs=placed,
         out_specs=(P("seq", ("group", "mp"), None), P("seq", ("group", "mp"), None)),

time: 172 us -> 41.3 us (0.24)
  blocking collectives: 78 us -> 0 us
  waiting for transfers between devices: 56.1 us -> 0 us
  Pallas kernels: 0 us -> 28 us
  between operations: 15.2 us -> 1.31 us
  matrix products: 8.57 us -> 0 us
  other arithmetic: 4.04 us -> 0 us
  local copies, waits for them, and re-layouts: 9.21 us -> 11.5 us
    unnamed x1 -> x0, blocking collectives: 61.1 us -> none
    pallas_call x0 -> x1, Pallas kernels: none -> 28 us  [fused(): pl.pallas_call(functools.partial(kernel, (n_group, n_seq, n_mp, n_chunk))...]
    all_gather x1 -> x0, waiting for transfers between devices: 25.4 us -> none  [local(): piece = lax.all_gather(rows, 'seq', axis=0, tiled=True)]
    psum x1 -> x0, waiting for transfers between devices: 18.6 us -> none  [local(): keys_vals = lax.psum(kv_part.astype(jnp.bfloat16), 'mp')]
    all_gather x1 -> x0, blocking collectives: 16.9 us -> none  [local(): block_lat = lax.all_gather(noised, ('group', 'mp'), axis=0, tiled=True)]
    reduce_scatter x1 -> x0, waiting for transfers between devices: 12.1 us -> none  [local(): lax.psum_scatter(query_part.astype(jnp.bfloat16), 'mp', scatter_dimension...]
    dot_general x6 -> x0, matrix products: 8.57 us -> none  [the longest x1 2.85 us: local(): jnp.dot(piece.reshape(-1, ds_loc), qkv_weight, preferred_element_type=jnp...]
    unnamed x17 -> x24, local copies, waits for them, and re-layouts: 7.3 us -> 11.5 us
  transfers between devices with their start and end apart: 3 -> 0, of which waited for: 3 -> 0; matrix products, arithmetic and copies ran while one was open for 5% -> 0% of each run, Pallas kernels for 0% -> 0%
where the time goes in v1:
time: 41.3 us; the launch traced here: 40.8 us
  Pallas kernels  28 us (68%)
  local copies, waits for them, and re-layouts  11.5 us (28%)
  between operations  1.31 us (3%)
    pallas_call x1, Pallas kernels, fused(): pl.pallas_call(functools.partial(kernel, (n_group, n_seq, n_mp, n_chunk))...  28 us
    unnamed x24, local copies, waits for them, and re-layouts  11.5 us

profile of v1, /device:TPU:0, one launch (start us, length us, event | category | flops | bytes accessed | tf_op | source)
XLA Modules:
  0.0 40.8 jit_solution(14697362755330661205)
XLA Ops:
  1.3 0.0 copy-start
  1.3 1.5 %copy-done = bf16[2560,3,1,128]{3,0,2,1:T(8,128)(2,1)S(1)} copy-done((bf16[2560,3,1,128]{3,0,2,1:T(8,128)(2,1)S(1)}, bf16[2560,3,1,128]{3,0,2,1:T(8,128)(2,1)}, u32[]{:S(2)}) %copy-start) | copy-done | bytes 1966104
  2.8 0.0 copy-start.1
  2.8 1.5 %copy-done.1 = bf16[2560,3,1,128]{3,0,2,1:T(8,128)(2,1)S(1)} copy-done((bf16[2560,3,1,128]{3,0,2,1:T(8,128)(2,1)S(1)}, bf16[2560,3,1,128]{3,0,2,1:T(8,128)(2,1)}, u32[]{:S(2)}) %copy-start.1) | copy-done | bytes 1966104
  4.4 0.0 copy-start.2
  4.4 1.0 %copy-done.2 = bf16[1,64,2560]{2,1,0:T(8,128)(2,1)S(1)} copy-done((bf16[1,64,2560]{2,1,0:T(8,128)(2,1)S(1)}, bf16[1,64,2560]{2,1,0:T(8,128)(2,1)}, u32[]{:S(2)}) %copy-start.2) | copy-done | bytes 327704
  5.3 0.0 copy-start.3
  5.3 1.0 %copy-done.3 = bf16[64,2560]{1,0:T(8,128)(2,1)S(1)} copy-done((bf16[64,2560]{1,0:T(8,128)(2,1)S(1)}, bf16[64,2560]{1,0:T(8,128)(2,1)}, u32[]{:S(2)}) %copy-start.3) | copy-done | bytes 327704
  6.3 0.0 copy-start.4
  6.3 0.9 %copy-done.4 = bf16[2048,64]{0,1:T(8,128)(2,1)S(1)} copy-done((bf16[2048,64]{0,1:T(8,128)(2,1)S(1)}, bf16[2048,64]{0,1:T(8,128)(2,1)}, u32[]{:S(2)}) %copy-start.4) | copy-done | bytes 262168
  7.3 0.0 copy-start.5
  7.3 0.8 %copy-done.5 = bf16[1,8,2048]{2,1,0:T(8,128)(2,1)S(1)} copy-done((bf16[1,8,2048]{2,1,0:T(8,128)(2,1)S(1)}, bf16[1,8,2048]{2,1,0:T(8,128)(2,1)}, u32[]{:S(2)}) %copy-start.5) | copy-done | bytes 32792
  8.0 0.0 copy-start.6
  8.0 0.7 %copy-done.6 = bf16[1,128,64]{1,2,0:T(8,128)(2,1)S(1)} copy-done((bf16[1,128,64]{1,2,0:T(8,128)(2,1)S(1)}, bf16[1,128,64]{1,2,0:T(8,128)(2,1)}, u32[]{:S(2)}) %copy-start.6) | copy-done | bytes 16408
  8.7 0.0 copy-start.7
  8.7 0.7 %copy-done.7 = bf16[1,128,64]{1,2,0:T(8,128)(2,1)S(1)} copy-done((bf16[1,128,64]{1,2,0:T(8,128)(2,1)S(1)}, bf16[1,128,64]{1,2,0:T(8,128)(2,1)}, u32[]{:S(2)}) %copy-start.7) | copy-done | bytes 16408
  9.5 0.0 copy-start.8
  9.5 0.7 %copy-done.8 = f32[1,2560]{1,0:T(1,128)S(1)} copy-done((f32[1,2560]{1,0:T(1,128)S(1)}, f32[1,2560]{1,0:T(1,128)}, u32[]{:S(2)}) %copy-start.8) | copy-done | bytes 10264
  10.2 0.0 copy-start.9
  10.2 0.7 %copy-done.9 = f32[2048]{0:T(1024)S(1)} copy-done((f32[2048]{0:T(1024)S(1)}, f32[2048]{0:T(1024)}, u32[]{:S(2)}) %copy-start.9) | copy-done | bytes 8216
  10.9 0.0 copy-start.10
  10.9 0.7 %copy-done.10 = f32[1,8,64]{2,1,0:T(8,128)S(1)} copy-done((f32[1,8,64]{2,1,0:T(8,128)S(1)}, f32[1,8,64]{2,1,0:T(8,128)}, u32[]{:S(2)}) %copy-start.10) | copy-done | bytes 2072
  11.6 28.0 %shard_map.131 = (f32[1,8,64]{2,1,0:T(8,128)S(1)}, bf16[1,8,2048]{2,1,0:T(8,128)(2,1)S(1)}) custom-call(bf16[1,8,2048]{2,1,0:T(8,128)(2,1)S(1)} %copy-done.5, f32[1,2048]{1,0:T(1,128)S(1)} %bitcast.15, bf16[64,2048]{1,0:T(8,128)(2,1)S(1)} %bitcast.12, f32[1,8,64]{2,1,0:T(8,128)S(1)} %copy-done.10, s32[1]{0:T(128)S(6)} %copy.16.time_ref, ...), custom_call_target="tpu_custom_call" | custom-call | tf_op jit(solution)/shard_map/pallas_call | solution.py:288
  39.5 0.6 %copy.17 = f32[1,8,64]{2,1,0:T(8,128)} copy(f32[1,8,64]{2,1,0:T(8,128)S(1)} %get-tuple-element.4) | data formatting | bytes 4096
  40.1 0.6 %copy.18 = bf16[1,8,2048]{2,1,0:T(8,128)(2,1)} copy(bf16[1,8,2048]{2,1,0:T(8,128)(2,1)S(1)} %get-tuple-element.5) | data formatting | bytes 65536
Async XLA Ops:
  1.3 1.5 %copy-start = (bf16[2560,3,1,128]{3,0,2,1:T(8,128)(2,1)S(1)}, bf16[2560,3,1,128]{3,0,2,1:T(8,128)(2,1)}, u32[]{:S(2)}) copy-start(bf16[2560,3,1,128]{3,0,2,1:T(8,128)(2,1)} %param.20) | copy-start | bytes 5898244
  2.8 1.5 %copy-start.1 = (bf16[2560,3,1,128]{3,0,2,1:T(8,128)(2,1)S(1)}, bf16[2560,3,1,128]{3,0,2,1:T(8,128)(2,1)}, u32[]{:S(2)}) copy-start(bf16[2560,3,1,128]{3,0,2,1:T(8,128)(2,1)} %param.22) | copy-start | bytes 5898244
  4.4 1.0 %copy-start.2 = (bf16[1,64,2560]{2,1,0:T(8,128)(2,1)S(1)}, bf16[1,64,2560]{2,1,0:T(8,128)(2,1)}, u32[]{:S(2)}) copy-start(bf16[1,64,2560]{2,1,0:T(8,128)(2,1)} %stream_ref.1) | copy-start | bytes 983044
  5.3 1.0 %copy-start.3 = (bf16[64,2560]{1,0:T(8,128)(2,1)S(1)}, bf16[64,2560]{1,0:T(8,128)(2,1)}, u32[]{:S(2)}) copy-start(bf16[64,2560]{1,0:T(8,128)(2,1)} %patch_ref.1) | copy-start | bytes 983044
  6.3 0.9 %copy-start.4 = (bf16[2048,64]{0,1:T(8,128)(2,1)S(1)}, bf16[2048,64]{0,1:T(8,128)(2,1)}, u32[]{:S(2)}) copy-start(bf16[2048,64]{0,1:T(8,128)(2,1)} %param.14) | copy-start | bytes 786436
  7.3 0.8 %copy-start.5 = (bf16[1,8,2048]{2,1,0:T(8,128)(2,1)S(1)}, bf16[1,8,2048]{2,1,0:T(8,128)(2,1)}, u32[]{:S(2)}) copy-start(bf16[1,8,2048]{2,1,0:T(8,128)(2,1)} %hid_ref.1) | copy-start | bytes 98308
  8.0 0.7 %copy-start.6 = (bf16[1,128,64]{1,2,0:T(8,128)(2,1)S(1)}, bf16[1,128,64]{1,2,0:T(8,128)(2,1)}, u32[]{:S(2)}) copy-start(bf16[1,128,64]{1,2,0:T(8,128)(2,1)} %param.21) | copy-start | bytes 49156
  8.7 0.7 %copy-start.7 = (bf16[1,128,64]{1,2,0:T(8,128)(2,1)S(1)}, bf16[1,128,64]{1,2,0:T(8,128)(2,1)}, u32[]{:S(2)}) copy-start(bf16[1,128,64]{1,2,0:T(8,128)(2,1)} %param.23) | copy-start | bytes 49156
  9.5 0.7 %copy-start.8 = (f32[1,2560]{1,0:T(1,128)S(1)}, f32[1,2560]{1,0:T(1,128)}, u32[]{:S(2)}) copy-start(f32[1,2560]{1,0:T(1,128)} %cond_ref.1) | copy-start | bytes 30724
  10.2 0.7 %copy-start.9 = (f32[2048]{0:T(1024)S(1)}, f32[2048]{0:T(1024)}, u32[]{:S(2)}) copy-start(f32[2048]{0:T(1024)} %param.13) | copy-start | bytes 24580
  10.9 0.7 %copy-start.10 = (f32[1,8,64]{2,1,0:T(8,128)S(1)}, f32[1,8,64]{2,1,0:T(8,128)}, u32[]{:S(2)}) copy-start(f32[1,8,64]{2,1,0:T(8,128)} %noise_ref.1) | copy-start | bytes 6148

commit v2 on v1

--- a/solution.py
+++ b/solution.py
@@ -17,20 +17,27 @@
 
 def kernel(
     sizes,
+    hid_hbm,
+    gain_hbm,
+    head_t_hbm,
+    noise_hbm,
+    time_ref,
+    stream_ref,
+    patch_hbm,
+    cond_ref,
+    teacher_ref,
+    teacher_out_hbm,
+    fake_ref,
+    fake_out_hbm,
+    gap_ref,
+    grad_ref,
     hid_ref,
     gain_ref,
     head_t_ref,
     noise_ref,
-    time_ref,
-    stream_ref,
     patch_ref,
-    cond_ref,
-    teacher_ref,
     teacher_out_ref,
-    fake_ref,
     fake_out_ref,
-    gap_ref,
-    grad_ref,
     latents,
     rows,
     conds,
@@ -41,6 +48,7 @@
     keys_vals,
     vel_out,
     vel_in,
+    small_sem,
     local_sem,
     lat_send,
     lat_recv,
@@ -92,6 +100,20 @@
         pl.semaphore_signal(barrier, inc=1, device_id=(at_group(d), s, m), device_id_type=MESH)
 
     my_rows = pl.ds(pl.multiple_of(g * share, share), share)
+    small = [
+        pltpu.make_async_copy(src, dst, small_sem.at[i])
+        for i, (src, dst) in enumerate(
+            (
+                (hid_hbm, hid_ref),
+                (gain_hbm, gain_ref),
+                (head_t_hbm, head_t_ref),
+                (noise_hbm, noise_ref),
+                (patch_hbm, patch_ref),
+                (teacher_out_hbm, teacher_out_ref),
+                (fake_out_hbm, fake_out_ref),
+            )
+        )
+    ]
     own = [
         pltpu.make_async_copy(stream_ref.at[0, my_rows, :], rows.at[s], local_sem.at[0]),
         pltpu.make_async_copy(cond_ref, conds.at[g], local_sem.at[1]),
@@ -100,8 +122,10 @@
         cols = pl.ds(j * head_dim, head_dim)
         own.append(pltpu.make_async_copy(fake_ref.at[j], w_fake.at[:, cols], local_sem.at[2 + j]))
         own.append(pltpu.make_async_copy(teacher_ref.at[j], w_teach.at[:, cols], local_sem.at[5 + j]))
-    for copy in own:
+    for copy in small[:4] + own[:2] + small[4:] + own[2:]:
         copy.start()
+    for copy in small[:4]:
+        copy.wait()
 
     hidden = hid_ref[0].astype(F32)
     gain = gain_ref[...]
@@ -144,7 +168,7 @@
     for copy in lat_copies:
         copy.wait_recv()
     lat_all = latents[...].reshape(tokens, -1).astype(BF16)
-    for copy in own:
+    for copy in own + small[4:]:
         copy.wait()
     for copy in cond_copies:
         copy.wait_recv()
@@ -282,7 +306,7 @@
     packed = 2 * tokens + queries
     n_plane = n_seq * n_mp - 1
     vmem = pl.BlockSpec(memory_space=pltpu.VMEM)
-    hbm = pl.BlockSpec(memory_space=pl.ANY)
+    hbm = pl.BlockSpec(memory_space=pltpu.HBM)
     smem = pl.BlockSpec(memory_space=pltpu.SMEM)
     dma = pltpu.SemaphoreType.DMA
     return pl.pallas_call(
@@ -291,9 +315,16 @@
             jax.ShapeDtypeStruct((1, per_dev, lat), F32),
             jax.ShapeDtypeStruct(gen_hidden.shape, BF16),
         ),
-        in_specs=[vmem, vmem, vmem, vmem, smem, hbm, vmem, vmem, hbm, vmem, hbm, vmem],
+        in_specs=[hbm] * 4 + [smem] + [hbm] * 7,
         out_specs=(vmem, vmem),
         scratch_shapes=[
+            pltpu.VMEM(gen_hidden.shape, BF16),
+            pltpu.VMEM((1, gen_hidden.shape[2]), F32),
+            pltpu.VMEM(head_weight.shape[::-1], BF16),
+            pltpu.VMEM(noise.shape, F32),
+            pltpu.VMEM(patch_weight.shape, BF16),
+            pltpu.VMEM((1, lat, head_dim), BF16),
+            pltpu.VMEM((1, lat, head_dim), BF16),
             pltpu.VMEM((n_seq, n_mp, per_dev, lat), F32),
             pltpu.VMEM((n_seq, share, ds_loc), BF16),
             pltpu.VMEM((n_group, 1, ds_loc), F32),
@@ -304,6 +335,7 @@
             pltpu.VMEM((EVALS, n_group, 2 * tokens, head_dim), BF16),
             pltpu.VMEM((n_seq, per_dev, lat), F32),
             pltpu.VMEM((n_seq, per_dev, lat), F32),
+            dma((7,)),
             dma((8,)),
             dma((n_plane,)),
             dma((n_plane,)),
@@ -319,7 +351,7 @@
             dma((n_seq - 1,)),
         ],
         compiler_params=pltpu.CompilerParams(
-            collective_id=0, has_side_effects=True, vmem_limit_bytes=40 * 1024 * 1024
+            collective_id=0, has_side_effects=True, vmem_limit_bytes=56 * 1024 * 1024
         ),
     )(
         gen_hidden,

time: 41.3 us -> 32.9 us (0.80)
  local copies, waits for them, and re-layouts: 11.5 us -> 2.65 us
  Pallas kernels: 28 us -> 28.8 us
    unnamed x24 -> x2, local copies, waits for them, and re-layouts: 11.5 us -> 2.65 us
    pallas_call x1, Pallas kernels: 28 us -> 28.8 us  [fused(): pl.pallas_call(functools.partial(kernel, (n_group, n_seq, n_mp, n_chunk))...]
where the time goes in v2:
time: 32.9 us; the launch traced here: 32.7 us
  Pallas kernels  28.8 us (88%)
  local copies, waits for them, and re-layouts  2.65 us (8%)
  between operations  1.29 us (4%)
    pallas_call x1, Pallas kernels, fused(): pl.pallas_call(functools.partial(kernel, (n_group, n_seq, n_mp, n_chunk))...  28.8 us
    unnamed x2, local copies, waits for them, and re-layouts  2.65 us

profile of v2, /device:TPU:0, one launch (start us, length us, event | category | flops | bytes accessed | tf_op | source)
XLA Modules:
  0.0 32.7 jit_solution(12774441816173391993)
XLA Ops:
  1.3 28.8 %shard_map.131 = (f32[1,8,64]{2,1,0:T(8,128)}, bf16[1,8,2048]{2,1,0:T(8,128)(2,1)}) custom-call(bf16[1,8,2048]{2,1,0:T(8,128)(2,1)} %hid_hbm.1, f32[1,2048]{1,0:T(1,128)} %bitcast.15, bf16[64,2048]{1,0:T(8,128)(2,1)} %bitcast.12, f32[1,8,64]{2,1,0:T(8,128)} %noise_hbm.1, s32[1]{0:T(128)S(6)} %copy.16.time_ref, bf16[1,64,2560]{2,1,0:T(8,128)(2,1)} %stream_ref.1, ...), custom_call_target="tpu_custom_call" | custom-call | tf_op jit(solution)/shard_map/pallas_call | solution.py:312
  30.1 1.3 %copy.17 = f32[1,8,64]{2,1,0:T(8,128)} copy(f32[1,8,64]{2,1,0:T(8,128)} %get-tuple-element.4) | data formatting | bytes 4096
  31.3 1.4 %copy.18 = bf16[1,8,2048]{2,1,0:T(8,128)(2,1)} copy(bf16[1,8,2048]{2,1,0:T(8,128)(2,1)} %get-tuple-element.5) | data formatting | bytes 65536

commit v3 on v2

--- a/solution.py
+++ b/solution.py
@@ -45,7 +45,6 @@
     w_teach,
     part_out,
     part_in,
-    keys_vals,
     vel_out,
     vel_in,
     small_sem,
@@ -58,8 +57,6 @@
     row_recv,
     part_send,
     part_recv,
-    kv_send,
-    kv_recv,
     vel_send,
     vel_recv,
 ):
@@ -96,8 +93,12 @@
     barrier = pltpu.get_barrier_semaphore()
     for ds, dm in plane:
         pl.semaphore_signal(barrier, inc=1, device_id=(g, at_seq(ds), at_mp(dm)), device_id_type=MESH)
-    for d in range(1, n_group):
-        pl.semaphore_signal(barrier, inc=1, device_id=(at_group(d), s, m), device_id_type=MESH)
+    cross = [(dg, ds, 0) for dg in range(1, n_group) for ds in range(n_seq)]
+    cross += [(dg, 0, dm) for dg in range(1, n_group) for dm in range(1, n_mp)]
+    for dg, ds, dm in cross:
+        pl.semaphore_signal(
+            barrier, inc=1, device_id=(at_group(dg), at_seq(ds), at_mp(dm)), device_id_type=MESH
+        )
 
     my_rows = pl.ds(pl.multiple_of(g * share, share), share)
     small = [
@@ -136,7 +137,7 @@
     noised = ((1.0 - sigma) * clean + sigma * noise_ref[0]).astype(BF16)
     latents[s, m] = noised.astype(F32)
 
-    pl.semaphore_wait(barrier, len(plane) + n_group - 1)
+    pl.semaphore_wait(barrier, len(plane) + len(cross))
 
     lat_copies = []
     for i, (ds, dm) in enumerate(plane):
@@ -189,90 +190,78 @@
         acc_teach = teach if c == 0 else acc_teach + teach
 
     partial = [acc_fake, acc_teach[:tokens], acc_teach[tokens:]]
-    part_copies = []
     for e in range(EVALS):
         q_part = partial[e][:, :head_dim].reshape(n_seq, n_mp, per_dev, head_dim)
         k_part = partial[e][:, head_dim : 2 * head_dim].astype(BF16)
         v_part = partial[e][:, 2 * head_dim :].astype(BF16)
-        for k in range(n_mp):
-            part_out[e, k, :tokens] = k_part
-            part_out[e, k, tokens : 2 * tokens] = v_part
-            part_out[e, k, 2 * tokens :] = q_part[:, k].reshape(queries, head_dim).astype(BF16)
-        part_copies.append(
-            [
-                push(
-                    part_out.at[e, at_mp(d)],
-                    part_in.at[e, d - 1],
-                    part_send.at[e, d - 1],
-                    part_recv.at[e, d - 1],
-                    (g, s, at_mp(d)),
-                )
-                for d in range(1, n_mp)
-            ]
-        )
-
-    kv_copies = []
-    queries_of = []
-    for e in range(EVALS):
-        total = part_out[e, m].astype(F32)
-        for d in range(1, n_mp):
-            part_copies[e][d - 1].wait_recv()
-            total = total + part_in[e, d - 1].astype(F32)
-        total = total.astype(BF16)
-        keys_vals[e, g] = total[: 2 * tokens]
-        queries_of.append(total[2 * tokens :])
-        kv_copies.append(
-            [
-                push(
-                    keys_vals.at[e, g],
-                    keys_vals.at[e, g],
-                    kv_send.at[e, d - 1],
-                    kv_recv.at[e, d - 1],
-                    (at_group(d), s, m),
-                )
-                for d in range(1, n_group)
-            ]
-        )
-
-    coeff = (1.0, -guidance, guidance - 1.0)
-    velocity = None
-    for e in range(EVALS):
-        for copy in kv_copies[e]:
-            copy.wait_recv()
-        keys = keys_vals[e, :, :tokens].reshape(n_group * tokens, head_dim)
-        values = keys_vals[e, :, tokens:].reshape(n_group * tokens, head_dim)
-        scores = lax.dot_general(
-            queries_of[e], keys, (((1,), (1,)), ((), ())), preferred_element_type=F32
-        ) / jnp.sqrt(F32(head_dim))
-        top = jnp.max(scores, axis=-1, keepdims=True)
-        expo = jnp.exp(scores - top)
-        probs = (expo / jnp.sum(expo, axis=-1, keepdims=True)).astype(BF16)
-        heads = jnp.dot(probs, values, preferred_element_type=F32).astype(BF16)
-        out_t = fake_out_ref[0] if e == 0 else teacher_out_ref[0]
-        term = coeff[e] * lax.dot_general(heads, out_t, (((1,), (1,)), ((), ())), preferred_element_type=F32)
-        velocity = term if e == 0 else velocity + term
-
-    vel_out[...] = velocity.reshape(n_seq, per_dev, -1)
+        for slot in (e,) if e < EVALS - 1 else range(e, n_group):
+            for k in range(n_mp):
+                part_out[slot, k, :tokens] = k_part
+                part_out[slot, k, tokens : 2 * tokens] = v_part
+                part_out[slot, k, 2 * tokens :] = q_part[:, k].reshape(queries, head_dim).astype(BF16)
+    part_copies = [
+        push(
+            part_out.at[at_group(dg), at_mp(dm)],
+            part_in.at[g, m],
+            part_send.at[dg, dm],
+            part_recv.at[dg, dm],
+            (at_group(dg), s, at_mp(dm)),
+        )
+        for dg in reversed(range(n_group))
+        for dm in reversed(range(n_mp))
+        if dg or dm
+    ]
+    part_in[g, m] = part_out[g, m]
+    is_fake = g == 0
+    out_t = jnp.where(is_fake, fake_out_ref[0], teacher_out_ref[0])
+    coeff = jnp.where(
+        is_fake, 1.0, jnp.where(g == 1, -guidance, jnp.where(g == 2, guidance - 1.0, 0.0))
+    )
+    for copy in part_copies:
+        copy.wait_recv()
+    total = part_in[:, 0].astype(F32)
+    for k in range(1, n_mp):
+        total = total + part_in[:, k].astype(F32)
+    total = total.astype(BF16)
+    keys = total[:, :tokens].reshape(n_group * tokens, head_dim)
+    values = total[:, tokens : 2 * tokens].reshape(n_group * tokens, head_dim)
+    asked = total[:, 2 * tokens :].reshape(n_group * queries, head_dim)
+    scores = lax.dot_general(
+        asked, keys, (((1,), (1,)), ((), ())), preferred_element_type=F32
+    ) / jnp.sqrt(F32(head_dim))
+    top = jnp.max(scores, axis=-1, keepdims=True)
+    expo = jnp.exp(scores - top)
+    probs = (expo / jnp.sum(expo, axis=-1, keepdims=True)).astype(BF16)
+    heads = jnp.dot(probs, values, preferred_element_type=F32).astype(BF16)
+    velocity = coeff * lax.dot_general(heads, out_t, (((1,), (1,)), ((), ())), preferred_element_type=F32)
+
+    vel_out[...] = velocity.reshape(n_group, n_seq, per_dev, -1)
     vel_copies = [
-        push(vel_out.at[at_seq(d)], vel_in.at[s], vel_send.at[d - 1], vel_recv.at[d - 1], (g, at_seq(d), m))
-        for d in range(1, n_seq)
+        push(
+            vel_out.at[at_group(dg), at_seq(ds)],
+            vel_in.at[g, s],
+            vel_send.at[dg, ds],
+            vel_recv.at[dg, ds],
+            (at_group(dg), at_seq(ds), m),
+        )
+        for ds in reversed(range(n_seq))
+        for dg in range(n_group)
+        if dg or ds
     ]
-    vel_in[s] = vel_out[s]
+    vel_in[g, s] = vel_out[g, s]
     scaled = hidden * rms
     for copy in vel_copies:
         copy.wait_recv()
-    gap = vel_in[0]
-    for k in range(1, n_seq):
-        gap = gap + vel_in[k]
+    gap = jnp.sum(vel_in[...].reshape(n_group * n_seq, per_dev, -1), axis=0)
     gap_ref[0] = gap
     grad_normed = jnp.dot(gap.astype(BF16), head_t_ref[...], preferred_element_type=F32)
     grad_gain = grad_normed * gain
     grad = rms * (grad_gain - scaled * jnp.mean(scaled * grad_gain, axis=-1, keepdims=True))
     grad_ref[0] = grad.astype(BF16)
 
-    for copy in lat_copies + cond_copies + vel_copies:
+    for copy in lat_copies + cond_copies + part_copies + vel_copies:
         copy.wait_send()
-    for copies in row_copies + part_copies + kv_copies:
+    for copies in row_copies:
         for copy in copies:
             copy.wait_send()
 
@@ -330,11 +319,10 @@
             pltpu.VMEM((n_group, 1, ds_loc), F32),
             pltpu.VMEM((ds_loc, width), BF16),
             pltpu.VMEM((ds_loc, width), BF16),
-            pltpu.VMEM((EVALS, n_mp, packed, head_dim), BF16),
-            pltpu.VMEM((EVALS, n_mp - 1, packed, head_dim), BF16),
-            pltpu.VMEM((EVALS, n_group, 2 * tokens, head_dim), BF16),
-            pltpu.VMEM((n_seq, per_dev, lat), F32),
-            pltpu.VMEM((n_seq, per_dev, lat), F32),
+            pltpu.VMEM((n_group, n_mp, packed, head_dim), BF16),
+            pltpu.VMEM((n_group, n_mp, packed, head_dim), BF16),
+            pltpu.VMEM((n_group, n_seq, per_dev, lat), F32),
+            pltpu.VMEM((n_group, n_seq, per_dev, lat), F32),
             dma((7,)),
             dma((8,)),
             dma((n_plane,)),
@@ -343,17 +331,17 @@
             dma((n_group - 1,)),
             dma((n_chunk, n_seq - 1)),
             dma((n_chunk, n_seq - 1)),
-            dma((EVALS, n_mp - 1)),
-            dma((EVALS, n_mp - 1)),
-            dma((EVALS, n_group - 1)),
-            dma((EVALS, n_group - 1)),
-            dma((n_seq - 1,)),
-            dma((n_seq - 1,)),
+            dma((n_group, n_mp)),
+            dma((n_group, n_mp)),
+            dma((n_group, n_seq)),
+            dma((n_group, n_seq)),
         ],
         compiler_params=pltpu.CompilerParams(
-            collective_id=0, has_side_effects=True, vmem_limit_bytes=56 * 1024 * 1024
+            collective_id=0, has_side_effects=True, vmem_limit_bytes=20 * 1024 * 1024
         ),
-    )(
+    )(*(
+        a if a.dtype == jnp.int32 else pltpu.with_memory_space_constraint(a, pltpu.HBM)
+        for a in (
         gen_hidden,
         gen_gain.reshape(1, -1),
         head_weight.T,
@@ -366,7 +354,8 @@
         teacher_out.transpose(0, 2, 1),
         fake_qkv[:, :, 0, :].transpose(1, 0, 2),
         fake_out.transpose(0, 2, 1),
-    )
+        )
+    ))
 
 
 def local(

time: 32.9 us -> 30.5 us (0.927)
  local copies, waits for them, and re-layouts: 2.65 us -> 1.21 us
  Pallas kernels: 28.8 us -> 27.9 us
    unnamed x2, local copies, waits for them, and re-layouts: 2.65 us -> 1.21 us
    pallas_call x1, Pallas kernels: 28.8 us -> 27.9 us  [fused(): pl.pallas_call(functools.partial(kernel, (n_group, n_seq, n_mp, n_chunk))...]
where the time goes in v3:
time: 30.5 us; the launch traced here: 30.4 us
  Pallas kernels  27.9 us (91%)
  between operations  1.29 us (4%)
  local copies, waits for them, and re-layouts  1.21 us (4%)
    pallas_call x1, Pallas kernels, fused(): pl.pallas_call(functools.partial(kernel, (n_group, n_seq, n_mp, n_chunk))...  27.9 us
    unnamed x2, local copies, waits for them, and re-layouts  1.21 us

profile of v3, /device:TPU:0, one launch (start us, length us, event | category | flops | bytes accessed | tf_op | source)
XLA Modules:
  0.0 30.4 jit_solution(5350889033488525103)
XLA Ops:
  1.3 27.9 %shard_map.131 = (f32[1,8,64]{2,1,0:T(8,128)S(1)}, bf16[1,8,2048]{2,1,0:T(8,128)(2,1)S(1)}) custom-call(bf16[1,8,2048]{2,1,0:T(8,128)(2,1)} %hid_hbm.1, f32[1,2048]{1,0:T(1,128)} %bitcast.15, bf16[64,2048]{1,0:T(8,128)(2,1)} %bitcast.12, f32[1,8,64]{2,1,0:T(8,128)} %noise_hbm.1, s32[1]{0:T(128)S(6)} %copy.16.time_ref, bf16[1,64,2560]{2,1,0:T(8,128)(2,1)} %stream_ref.1, ...), custom_call_target="tpu_custom_call" | custom-call | tf_op jit(solution)/shard_map/pallas_call | solution.py:301
  29.2 0.6 %copy.17 = f32[1,8,64]{2,1,0:T(8,128)} copy(f32[1,8,64]{2,1,0:T(8,128)S(1)} %get-tuple-element.4) | data formatting | bytes 4096
  29.8 0.6 %copy.18 = bf16[1,8,2048]{2,1,0:T(8,128)(2,1)} copy(bf16[1,8,2048]{2,1,0:T(8,128)(2,1)S(1)} %get-tuple-element.5) | data formatting | bytes 65536

commit v4 on v3

--- a/solution.py
+++ b/solution.py
@@ -13,6 +13,12 @@
 F32 = jnp.float32
 BF16 = jnp.bfloat16
 EVALS = 3
+
+
+def run_if(needed, action):
+    @pl.when(needed)
+    def _():
+        action()
 
 
 def kernel(
@@ -55,6 +61,7 @@
     cond_recv,
     row_send,
     row_recv,
+    hand_send,
     part_send,
     part_recv,
     vel_send,
@@ -83,11 +90,14 @@
 
     plane = [(ds, dm) for ds in range(n_seq) for dm in range(n_mp) if ds or dm]
 
-    def push(src, dst, send, recv, device):
+    def push(src, dst, send, recv, device, needed=None):
         copy = pltpu.make_async_remote_copy(
             src_ref=src, dst_ref=dst, send_sem=send, recv_sem=recv, device_id=device, device_id_type=MESH
         )
-        copy.start()
+        if needed is None:
+            copy.start()
+        else:
+            run_if(needed, copy.start)
         return copy
 
     barrier = pltpu.get_barrier_semaphore()
@@ -144,6 +154,11 @@
         lat_copies.append(
             push(latents.at[s, m], latents.at[s, m], lat_send.at[i], lat_recv.at[i], (g, at_seq(ds), at_mp(dm)))
         )
+    direct = [jnp.abs(at_seq(d) - s) != n_seq - 1 for d in range(1, n_seq)]
+    inner = jnp.logical_and(s > 0, s < n_seq - 1)
+    onward = lax.rem(3 * s + 5, n_seq)
+    onward_recv = lax.rem(2 * s + 2, n_seq)
+    handed = []
     cond_copies = []
     row_copies = []
     for c in range(n_chunk):
@@ -157,6 +172,7 @@
                     row_send.at[c, d - 1],
                     row_recv.at[c, d - 1],
                     (g, at_seq(d), m),
+                    direct[d - 1],
                 )
             )
         row_copies.append(group_of)
@@ -178,8 +194,19 @@
     acc_teach = None
     for c in range(n_chunk):
         cols = pl.ds(c * chunk, chunk)
-        for copy in row_copies[c]:
-            copy.wait_recv()
+        row_copies[c][1].wait_recv()
+        handed.append(
+            push(
+                rows.at[at_seq(2), :, cols],
+                rows.at[at_seq(2), :, cols],
+                hand_send.at[c],
+                row_recv.at[c, onward_recv],
+                (g, onward, m),
+                inner,
+            )
+        )
+        row_copies[c][0].wait_recv()
+        row_copies[c][2].wait_recv()
         base = rows[:, :, cols].reshape(tokens, chunk).astype(F32) + jnp.dot(
             lat_all, patch_ref[:, cols], preferred_element_type=F32
         )
@@ -262,8 +289,10 @@
     for copy in lat_copies + cond_copies + part_copies + vel_copies:
         copy.wait_send()
     for copies in row_copies:
-        for copy in copies:
-            copy.wait_send()
+        for needed, copy in zip(direct, copies):
+            run_if(needed, copy.wait_send)
+    for copy in handed:
+        run_if(inner, copy.wait_send)
 
 
 def fused(
@@ -331,6 +360,7 @@
             dma((n_group - 1,)),
             dma((n_chunk, n_seq - 1)),
             dma((n_chunk, n_seq - 1)),
+            dma((n_chunk,)),
             dma((n_group, n_mp)),
             dma((n_group, n_mp)),
             dma((n_group, n_seq)),
@@ -449,7 +479,7 @@
     def part(*arrays):
         per_dev, ds_loc = arrays[0].shape[1], arrays[5].shape[2]
         tiled = per_dev % 8 == 0 and n_mp * per_dev % 16 == 0 and n_seq * per_dev % 16 == 0
-        small = n_group > 1 and n_seq > 1 and n_mp > 1 and n_group >= EVALS
+        small = n_group > 1 and n_seq == 4 and n_mp > 1 and n_group >= EVALS
         if tiled and small and ds_loc % 512 == 0:
             return fused(*arrays)
         return local(*arrays)

time: 30.5 us -> 30 us (0.984)
  Pallas kernels: 27.9 us -> 27.4 us
    pallas_call x1, Pallas kernels: 27.9 us -> 27.4 us  [fused(): pl.pallas_call(functools.partial(kernel, (n_group, n_seq, n_mp, n_chunk))...]
where the time goes in v4:
time: 30 us; the launch traced here: 29.9 us
  Pallas kernels  27.4 us (91%)
  between operations  1.29 us (4%)
  local copies, waits for them, and re-layouts  1.21 us (4%)
    pallas_call x1, Pallas kernels, fused(): pl.pallas_call(functools.partial(kernel, (n_group, n_seq, n_mp, n_chunk))...  27.4 us
    unnamed x2, local copies, waits for them, and re-layouts  1.21 us

profile of v4, /device:TPU:0, one launch (start us, length us, event | category | flops | bytes accessed | tf_op | source)
XLA Modules:
  0.0 29.9 jit_solution(6471563302058684347)
XLA Ops:
  1.3 27.4 %shard_map.131 = (f32[1,8,64]{2,1,0:T(8,128)S(1)}, bf16[1,8,2048]{2,1,0:T(8,128)(2,1)S(1)}) custom-call(bf16[1,8,2048]{2,1,0:T(8,128)(2,1)} %hid_hbm.1, f32[1,2048]{1,0:T(1,128)} %bitcast.15, bf16[64,2048]{1,0:T(8,128)(2,1)} %bitcast.12, f32[1,8,64]{2,1,0:T(8,128)} %noise_hbm.1, s32[1]{0:T(128)S(6)} %copy.16.time_ref, bf16[1,64,2560]{2,1,0:T(8,128)(2,1)} %stream_ref.1, ...), custom_call_target="tpu_custom_call" | custom-call | tf_op jit(solution)/shard_map/pallas_call | solution.py:330
  28.7 0.6 %copy.17 = f32[1,8,64]{2,1,0:T(8,128)} copy(f32[1,8,64]{2,1,0:T(8,128)S(1)} %get-tuple-element.4) | data formatting | bytes 4096
  29.3 0.6 %copy.18 = bf16[1,8,2048]{2,1,0:T(8,128)(2,1)} copy(bf16[1,8,2048]{2,1,0:T(8,128)(2,1)S(1)} %get-tuple-element.5) | data formatting | bytes 65536
